TPU v7x, 128 devices: a whole 4x4x4 slice. The times are simulated.
128 devices in a mesh: dp: 8 (over z_hi, x), tensor: 16 (over y, z_lo, core).
Axes of the slice: x: 4, y: 4, z: 4 (z_hi: 2, z_lo: 2; z = z_hi * 2 + z_lo), core: 2. Of those that a mesh axis runs over, the one named last changes fastest.
Arguments:
- inputs: bfloat16 [16, 1024, 2048], P('dp', 'tensor'), may hold values from -6 to 6
- teacher: bfloat16 [16, 1024, 2048], P('dp', 'tensor'), may hold values from -6 to 6
- segment_ids: int32 [16, 1024], P('dp'), may hold values from 0 to 3, never falling along the last dimension, each value on 1 to 512 neighbouring positions
- padding: int32 [16, 1024], P('dp', 'tensor'), may hold values from 0 to 1, as said below
- attn_gain: float32 [2048], replicated, may hold values from 0.5 to 1.5
- qkv_weight: bfloat16 [2048, 3, 2048], P('dp', None, 'tensor'), may hold values from -0.125 to 0.125
- beta_weight: bfloat16 [2048, 16], P('dp', 'tensor'), may hold values from -0.125 to 0.125
- conv_taps: bfloat16 [4, 3, 16, 128], P(None, None, 'tensor', 'dp'), may hold values from -4 to 4
- head_gain: bfloat16 [16, 128], P('tensor', 'dp'), may hold values from 0.5 to 1.5
- out_weight: bfloat16 [2048, 2048], P('tensor', 'dp'), may hold values from -0.125 to 0.125
- mlp_gain: float32 [2048], replicated, may hold values from 0.5 to 1.5
- gate_weight: bfloat16 [2048, 5632], P('dp', 'tensor'), may hold values from -0.125 to 0.125
- up_weight: bfloat16 [2048, 5632], P('dp', 'tensor'), may hold values from -0.125 to 0.125
- down_weight: bfloat16 [5632, 2048], P('tensor', 'dp'), may hold values from -0.15625 to 0.15625
Outputs:
- block_out: bfloat16 [16, 1024, 2048], P('dp', 'tensor')
- loss: float32 [], replicated
- input_grad: float32 [16, 1024, 2048], P('dp', 'tensor')
- attn_gain_grad: float32 [2048], replicated
- qkv_grad: float32 [2048, 3, 2048], P('dp', None, 'tensor')
- beta_grad: float32 [2048, 16], P('dp', 'tensor')
- taps_grad: float32 [4, 3, 16, 128], P(None, None, 'tensor', 'dp')
- head_gain_grad: float32 [16, 128], P('tensor', 'dp')
- out_grad: float32 [2048, 2048], P('tensor', 'dp')
- mlp_gain_grad: float32 [2048], replicated
- gate_grad: float32 [2048, 5632], P('dp', 'tensor')
- up_grad: float32 [2048, 5632], P('dp', 'tensor')
- down_grad: float32 [5632, 2048], P('tensor', 'dp')
Inputs may be any that keep to these rules, and one draw needn't show every extreme that they name: `padding`: in each sequence the tokens that count form a leading run of 256 to 767 tokens; the rest are 0. `segment_ids`: document numbers never fall along a sequence; a document has 1 to 512 tokens.
All inputs are finite; a program needn't handle non-finite values.
Results may differ from a plain program's by a relative error of at most 0.029.
Values may be sent and summed in bfloat16 or wider, within the bound.
A program may use at most 192 MiB of HBM per device.

v0:
```python
import jax
import jax.numpy as jnp
from jax import lax
from jax.sharding import PartitionSpec as P

GROUP = 64
highest = lax.Precision.HIGHEST


def rms_norm(values, epsilon):
    return values * lax.rsqrt(jnp.mean(values * values, -1, keepdims=True) + epsilon)


def unit_norm(values):
    return values * lax.rsqrt(jnp.sum(values * values, -1, keepdims=True) + 1e-06)


def short_conv(fields, taps, segment):
    length = fields.shape[0]
    total = fields * taps[0]
    for offset in range(1, taps.shape[0]):
        blank_rows = jnp.zeros((offset,) + fields.shape[1:], fields.dtype)
        moved = jnp.concatenate([blank_rows, fields[: length - offset]], 0)
        earlier = jnp.concatenate(
            [jnp.full((offset,), -1, jnp.int32), segment[: length - offset]], 0
        )
        keep = (earlier == segment).astype(fields.dtype)
        total = total + moved * keep[:, None, None, None] * taps[offset]
    return total


def delta_block(carry, block):
    state, previous = carry
    query, keys, values, beta, segment = block
    size = segment.shape[0]
    dtype = state.dtype
    carried = (segment == previous).astype(dtype)
    same = (segment[:, None] == segment[None, :]).astype(dtype)
    strict = jnp.tril(jnp.ones((size, size), dtype), -1)
    within = jnp.tril(jnp.ones((size, size), dtype))
    gram = jnp.einsum("htk,hsk->hts", keys, keys, precision=highest)
    mixing = gram * beta[:, None, :] * (same * strict)
    recalled = jnp.einsum("htk,hvk->htv", keys, state, precision=highest)
    target = values - carried[None, :, None] * recalled
    system = jnp.eye(size, dtype=dtype)[None] + mixing
    updates = jax.vmap(
        lambda matrix, right: jax.scipy.linalg.solve_triangular(
            matrix, right, lower=True, unit_diagonal=True
        )
    )(system, target)
    weighted = updates * beta[:, :, None]
    scores = jnp.einsum("htk,hsk->hts", query, keys, precision=highest) * (same * within)
    output = carried[None, :, None] * jnp.einsum("htk,hvk->htv", query, state, precision=highest)
    output = output + jnp.einsum("hts,hsv->htv", scores, weighted, precision=highest)
    closing = (segment == segment[size - 1]).astype(dtype)
    new_state = carried[size - 1] * state + jnp.einsum(
        "hsv,hsk->hvk", weighted * closing[None, :, None], keys, precision=highest
    )
    return ((new_state, segment[size - 1]), output)


def mixer(projected, beta_logit, taps, head_gain, segment):
    length = projected.shape[0]
    heads = beta_logit.shape[1]
    width = taps.shape[-1]
    fields = projected.reshape(length, 3, heads, width)
    mixed = jax.nn.silu(short_conv(fields, taps, segment))
    query = unit_norm(mixed[:, 0]) * width ** (-0.5)
    keys = unit_norm(mixed[:, 1])
    values = mixed[:, 2]
    beta = jax.nn.sigmoid(beta_logit)
    blocks = length // GROUP

    def arrange(array):
        return jnp.transpose(array.reshape(blocks, GROUP, heads, width), (0, 2, 1, 3))

    beta_blocks = jnp.transpose(beta.reshape(blocks, GROUP, heads), (0, 2, 1))
    segment_blocks = segment.reshape(blocks, GROUP)
    start = (jnp.zeros((heads, width, width), projected.dtype), jnp.int32(-1))
    final, outputs = lax.scan(
        jax.checkpoint(delta_block),
        start,
        (arrange(query), arrange(keys), arrange(values), beta_blocks, segment_blocks),
    )
    raw = jnp.transpose(outputs, (0, 2, 1, 3)).reshape(length, heads, width)
    normed = rms_norm(raw, 1e-05) * head_gain
    return normed.reshape(length, heads * width)


def fetch(
    qkv_weight, beta_weight, conv_taps, head_gain, out_weight, gate_weight, up_weight, down_weight
):
    return (
        lax.all_gather(qkv_weight, "dp", axis=0, tiled=True),
        lax.all_gather(beta_weight, "dp", axis=0, tiled=True),
        lax.all_gather(conv_taps, "dp", axis=3, tiled=True),
        lax.all_gather(head_gain, "dp", axis=1, tiled=True),
        lax.all_gather(out_weight, "dp", axis=1, tiled=True),
        lax.all_gather(gate_weight, "dp", axis=0, tiled=True),
        lax.all_gather(up_weight, "dp", axis=0, tiled=True),
        lax.all_gather(down_weight, "dp", axis=1, tiled=True),
    )


def settle(qkv_part, beta_part, taps_part, gain_part, out_part, gate_part, up_part, down_part):
    return (
        lax.psum_scatter(
            qkv_part.astype(jnp.bfloat16), "dp", scatter_dimension=0, tiled=True
        ).astype(jnp.float32),
        lax.psum_scatter(
            beta_part.astype(jnp.bfloat16), "dp", scatter_dimension=0, tiled=True
        ).astype(jnp.float32),
        lax.psum_scatter(
            taps_part.astype(jnp.bfloat16), "dp", scatter_dimension=3, tiled=True
        ).astype(jnp.float32),
        lax.psum_scatter(
            gain_part.astype(jnp.bfloat16), "dp", scatter_dimension=1, tiled=True
        ).astype(jnp.float32),
        lax.psum_scatter(
            out_part.astype(jnp.bfloat16), "dp", scatter_dimension=1, tiled=True
        ).astype(jnp.float32),
        lax.psum_scatter(
            gate_part.astype(jnp.bfloat16), "dp", scatter_dimension=0, tiled=True
        ).astype(jnp.float32),
        lax.psum_scatter(
            up_part.astype(jnp.bfloat16), "dp", scatter_dimension=0, tiled=True
        ).astype(jnp.float32),
        lax.psum_scatter(
            down_part.astype(jnp.bfloat16), "dp", scatter_dimension=1, tiled=True
        ).astype(jnp.float32),
    )


def widened(array, dim, factor):
    shape = list(array.shape)
    shape[dim] = shape[dim] * factor
    return jnp.zeros(tuple(shape), jnp.float32)


def body(
    inputs,
    teacher,
    segment_ids,
    padding,
    attn_gain,
    qkv_weight,
    beta_weight,
    conv_taps,
    head_gain,
    out_weight,
    mlp_gain,
    gate_weight,
    up_weight,
    down_weight,
):
    length = segment_ids.shape[1]
    dp_count = lax.axis_size("dp")
    all_rows = inputs.shape[0] * length * dp_count
    valid = lax.psum(jnp.sum(padding), ("dp", "tensor"))
    scale = all_rows / valid.astype(jnp.float32)
    shards = (
        qkv_weight,
        beta_weight,
        conv_taps,
        head_gain,
        out_weight,
        gate_weight,
        up_weight,
        down_weight,
    )
    gather_dims = (0, 0, 3, 1, 1, 0, 0, 1)
    totals = tuple((widened(weight, dim, dp_count) for weight, dim in zip(shards, gather_dims)))
    zero_gain = jnp.zeros(attn_gain.shape, jnp.float32)

    def micro_step(carry, batch):
        totals, squares, attn_sum, mlp_sum = carry
        tokens, target, segment, mask = batch
        weights_now = fetch(
            qkv_weight,
            beta_weight,
            conv_taps,
            head_gain,
            out_weight,
            gate_weight,
            up_weight,
            down_weight,
        )
        qkv_full, beta_full, taps_full, gain_full, out_full, gate_full, up_full, down_full = (
            weights_now
        )
        tokens32 = tokens.astype(jnp.float32)
        attn_scale = lax.rsqrt(jnp.mean(tokens32 * tokens32, -1, keepdims=True) + 1e-06)
        attn_unit = tokens32 * attn_scale
        normed = (attn_unit * attn_gain).astype(jnp.bfloat16)
        gathered = lax.all_gather(normed, "tensor", axis=0, tiled=True)
        projected = jnp.einsum(
            "sd,dcf->scf", gathered, qkv_full, preferred_element_type=jnp.float32
        )
        beta_logit = jnp.dot(gathered, beta_full, preferred_element_type=jnp.float32)

        def local_mixer(projected_in, beta_in, taps_in, gain_in):
            return mixer(projected_in, beta_in, taps_in, gain_in, segment)

        heads_out, mixer_back = jax.vjp(
            local_mixer,
            projected,
            beta_logit,
            taps_full.astype(jnp.float32),
            gain_full.astype(jnp.float32),
        )
        heads_low = heads_out.astype(jnp.bfloat16)
        attention = lax.psum_scatter(
            jnp.dot(heads_low, out_full, preferred_element_type=jnp.float32).astype(jnp.bfloat16),
            "tensor",
            scatter_dimension=0,
            tiled=True,
        ).astype(jnp.float32)
        hidden = tokens32 + attention
        mlp_scale = lax.rsqrt(jnp.mean(hidden * hidden, -1, keepdims=True) + 1e-06)
        mlp_unit = hidden * mlp_scale
        ffn_in = (mlp_unit * mlp_gain).astype(jnp.bfloat16)
        ffn_all = lax.all_gather(ffn_in, "tensor", axis=0, tiled=True)
        gate = jnp.dot(ffn_all, gate_full, preferred_element_type=jnp.float32)
        up = jnp.dot(ffn_all, up_full, preferred_element_type=jnp.float32)
        sigma = jax.nn.sigmoid(gate)
        act = (gate * sigma * up).astype(jnp.bfloat16)
        output = hidden + lax.psum_scatter(
            jnp.dot(act, down_full, preferred_element_type=jnp.float32).astype(jnp.bfloat16),
            "tensor",
            scatter_dimension=0,
            tiled=True,
        ).astype(jnp.float32)
        diff = output - target.astype(jnp.float32)
        mask32 = mask.astype(jnp.float32)
        squares = squares + jnp.sum(jnp.sum(diff * diff, -1) * mask32)
        block_grad = (scale * mask32)[:, None] * diff
        weights_back = fetch(
            qkv_weight,
            beta_weight,
            conv_taps,
            head_gain,
            out_weight,
            gate_weight,
            up_weight,
            down_weight,
        )
        qkv_back, beta_back, taps_back, gain_back, out_back, gate_back, up_back, down_back = (
            weights_back
        )
        ffn_grad_all = lax.all_gather(block_grad.astype(jnp.bfloat16), "tensor", axis=0, tiled=True)
        down_part = jnp.einsum("sf,sd->fd", act, ffn_grad_all, preferred_element_type=jnp.float32)
        act_grad = jnp.einsum(
            "sd,fd->sf", ffn_grad_all, down_back, preferred_element_type=jnp.float32
        )
        gate_low = (act_grad * up * sigma * (1.0 + gate * (1.0 - sigma))).astype(jnp.bfloat16)
        up_low = (act_grad * gate * sigma).astype(jnp.bfloat16)
        gate_part = jnp.einsum("sd,sf->df", ffn_all, gate_low, preferred_element_type=jnp.float32)
        up_part = jnp.einsum("sd,sf->df", ffn_all, up_low, preferred_element_type=jnp.float32)
        total = jnp.einsum("sf,df->sd", gate_low, gate_back, preferred_element_type=jnp.float32)
        mlp_grad = lax.psum_scatter(
            (
                total + jnp.einsum("sf,df->sd", up_low, up_back, preferred_element_type=jnp.float32)
            ).astype(jnp.bfloat16),
            "tensor",
            scatter_dimension=0,
            tiled=True,
        ).astype(jnp.float32)
        mlp_sum = mlp_sum + jnp.sum(mlp_grad * mlp_unit, 0)
        mlp_inner = mlp_grad * mlp_gain
        hidden_grad = block_grad + mlp_scale * (
            mlp_inner - mlp_unit * jnp.mean(mlp_inner * mlp_unit, -1, keepdims=True)
        )
        attention_all = lax.all_gather(
            hidden_grad.astype(jnp.bfloat16), "tensor", axis=0, tiled=True
        )
        out_part = jnp.einsum(
            "sf,sd->fd", heads_low, attention_all, preferred_element_type=jnp.float32
        )
        heads_grad = jnp.einsum(
            "sd,fd->sf", attention_all, out_back, preferred_element_type=jnp.float32
        )
        projected_grad, beta_logit_grad, taps_part, gain_part = mixer_back(heads_grad)
        projected_low = projected_grad.astype(jnp.bfloat16)
        beta_low = beta_logit_grad.astype(jnp.bfloat16)
        qkv_part = jnp.einsum(
            "sd,scf->dcf", gathered, projected_low, preferred_element_type=jnp.float32
        )
        beta_part = jnp.einsum("sd,sh->dh", gathered, beta_low, preferred_element_type=jnp.float32)
        total = jnp.einsum(
            "scf,dcf->sd", projected_low, qkv_back, preferred_element_type=jnp.float32
        )
        normed_grad = lax.psum_scatter(
            (
                total
                + jnp.einsum("sh,dh->sd", beta_low, beta_back, preferred_element_type=jnp.float32)
            ).astype(jnp.bfloat16),
            "tensor",
            scatter_dimension=0,
            tiled=True,
        ).astype(jnp.float32)
        attn_sum = attn_sum + jnp.sum(normed_grad * attn_unit, 0)
        attn_inner = normed_grad * attn_gain
        input_grad = hidden_grad + attn_scale * (
            attn_inner - attn_unit * jnp.mean(attn_inner * attn_unit, -1, keepdims=True)
        )
        parts = (qkv_part, beta_part, taps_part, gain_part, out_part, gate_part, up_part, down_part)
        totals = tuple((old + new for old, new in zip(totals, parts)))
        return ((totals, squares, attn_sum, mlp_sum), (output.astype(jnp.bfloat16), input_grad))

    start = (totals, jnp.zeros((), jnp.float32), zero_gain, zero_gain)
    finals, outputs = lax.scan(micro_step, start, (inputs, teacher, segment_ids, padding))
    totals, squares, attn_sum, mlp_sum = finals
    block_out, input_grad = outputs
    totals = settle(
        totals[0], totals[1], totals[2], totals[3], totals[4], totals[5], totals[6], totals[7]
    )
    attn_total, mlp_total, square_total = lax.psum((attn_sum, mlp_sum, squares), ("dp", "tensor"))
    loss = square_total / (valid.astype(jnp.float32) * inputs.shape[2])
    return (
        block_out,
        loss,
        input_grad,
        attn_total,
        totals[0],
        totals[1],
        totals[2],
        totals[3],
        totals[4],
        mlp_total,
        totals[5],
        totals[6],
        totals[7],
    )


def solution(mesh):
    in_specs = (
        P("dp", "tensor", None),
        P("dp", "tensor", None),
        P("dp", None),
        P("dp", "tensor"),
        P(),
        P("dp", None, "tensor"),
        P("dp", "tensor"),
        P(None, None, "tensor", "dp"),
        P("tensor", "dp"),
        P("tensor", "dp"),
        P(),
        P("dp", "tensor"),
        P("dp", "tensor"),
        P("tensor", "dp"),
    )
    out_specs = (
        P("dp", "tensor", None),
        P(),
        P("dp", "tensor", None),
        P(),
        P("dp", None, "tensor"),
        P("dp", "tensor"),
        P(None, None, "tensor", "dp"),
        P("tensor", "dp"),
        P("tensor", "dp"),
        P(),
        P("dp", "tensor"),
        P("dp", "tensor"),
        P("tensor", "dp"),
    )
    return jax.shard_map(body, mesh=mesh, in_specs=in_specs, out_specs=out_specs, check_vma=False)
```

profile of v0, /device:TPU:0, one launch (start us, length us, event | category | flops | bytes accessed | tf_op | source)
XLA Modules:
  0.0 3572.0 jit_solution(11940812805327868886)
XLA Ops:
  9.4 68.2 %psum.28 = s32[]{:T(128)} all-reduce(s32[]{:T(128)} %reduce_sum.286), channel_id=1, replica_groups=mesh['dp'=8,'tensor'=16] {'dp','tensor'}, use_global_device_ids=true, to_apply=%region_1.0 | all-reduce | flops 1 | bytes 8 | tf_op jit(solution)/shard_map/psum | solution.py:159
  79.7 2898.0 %while.135 = (s32[]{:T(128)}, f32[2048,3,128]{2,0,1:T(8,128)}, f32[2048,1]{0,1:T(1,128)}, f32[4,3,1,128]{3,2,1,0:T(1,128)}, f32[1,128]{1,0:T(1,128)}, /*index=5*...) while((s32[]{:T(128)}, f32[2048,3,128]{2,0,1:T(8,128)}, ...), condition=%wide.region_32.34_spmd.clone, body=%wide.region_2.33_spmd.clone.sunk | while | flops 20024219648 | bytes 558299264 | solution.py:311
  220.5 276.7 %while.136 = (s32[]{:T(128)}, f32[1,128,128]{2,1,0:T(8,128)S(1)}, s32[]{:T(128)}, f32[16,1,64,128]{3,2,1,0:T(8,128)}, f32[16,1,128,128]{3,2,1,0:T(8,128)}, /*ind...) while((s32[]{:T(128)}, f32[1,128,128]{2,1,0:T(8,128)S(1)}, ...), condition=%wide.region_7.8_spmd.clone, body=%wide.region_6.7_spmd.clone.sunk | while | flops 63140160 | bytes 960217 | solution.py:80
  505.5 63.9 %reduce-scatter.35.cloned.1.call-done = bf16[64,2048]{1,0:T(8,128)(2,1)} async-done(((bf16[1024,2048]{1,0:T(8,128)(2,1)}), bf16[64,2048]{1,0:T(8,128)(2,1)}) %reduce-scatter.35.cloned.1.call-update) | async-done | bytes 262160 | tf_op jit(solution)/shard_map/while/body/eval_jaxpr/reduce_scatter | solution.py:212
  574.1 47.6 %all-gather.15.cloned.1.call-done = bf16[2048,352]{0,1:T(8,128)(2,1)} async-done(((bf16[256,352]{0,1:T(8,128)(2,1)}), bf16[2048,352]{0,1:T(8,128)(2,1)}) %all-gather.15.cloned.1.call-update) | async-done | bytes 1441808 | tf_op jit(solution)/shard_map/while/body/eval_jaxpr/all_gather | solution.py:99
  665.5 48.5 %all-gather.17.cloned.1.call-done = bf16[2048,352]{0,1:T(8,128)(2,1)} async-done(((bf16[256,352]{0,1:T(8,128)(2,1)}), bf16[2048,352]{0,1:T(8,128)(2,1)}) %all-gather.17.cloned.1.call-update) | async-done | bytes 1441808 | tf_op jit(solution)/shard_map/while/body/eval_jaxpr/all_gather | solution.py:100
  720.2 46.5 %all-gather.19.cloned.1.call-done = bf16[352,2048]{1,0:T(8,128)(2,1)} async-done(((bf16[352,256]{1,0:T(8,128)(2,1)}), bf16[352,2048]{1,0:T(8,128)(2,1)}) %all-gather.19.cloned.1.call-update) | async-done | bytes 1441808 | tf_op jit(solution)/shard_map/while/body/eval_jaxpr/all_gather | solution.py:101
  773.4 65.7 %reduce-scatter.37.cloned.1.call-done = bf16[64,2048]{1,0:T(8,128)(2,1)} async-done(((bf16[1024,2048]{1,0:T(8,128)(2,1)}), bf16[64,2048]{1,0:T(8,128)(2,1)}) %reduce-scatter.37.cloned.1.call-update) | async-done | bytes 262160 | tf_op jit(solution)/shard_map/while/body/eval_jaxpr/reduce_scatter | solution.py:227
  890.6 67.3 %reduce-scatter.39.cloned.1.call-done = bf16[64,2048]{1,0:T(8,128)(2,1)} async-done(((bf16[1024,2048]{1,0:T(8,128)(2,1)}), bf16[64,2048]{1,0:T(8,128)(2,1)}) %reduce-scatter.39.cloned.1.call-update) | async-done | bytes 262160 | tf_op jit(solution)/shard_map/while/body/eval_jaxpr/reduce_scatter | solution.py:260
  1007.3 429.0 %while.137 = (s32[]{:T(128)}, f32[1,128,128]{2,1,0:T(8,128)S(1)}, f32[16,1,64,128]{3,2,1,0:T(8,128)}, f32[16,1,64,128]{3,2,1,0:T(8,128)}, f32[16,1,64,128]{3,2,1...) while((s32[]{:T(128)}, f32[1,128,128]{2,1,0:T(8,128)S(1)}, ...), condition=%wide.region_18.19_spmd.clone, body=%wide.region_15.18_spmd.clone.sunk | while | flops 160874752 | bytes 2876935 | solution.py:80
  1669.5 276.7 %while.136 = (s32[]{:T(128)}, f32[1,128,128]{2,1,0:T(8,128)S(1)}, s32[]{:T(128)}, f32[16,1,64,128]{3,2,1,0:T(8,128)}, f32[16,1,128,128]{3,2,1,0:T(8,128)}, /*ind...) while((s32[]{:T(128)}, f32[1,128,128]{2,1,0:T(8,128)S(1)}, ...), condition=%wide.region_7.8_spmd.clone, body=%wide.region_6.7_spmd.clone.sunk | while | flops 63140160 | bytes 960217 | solution.py:80
  1954.4 62.5 %reduce-scatter.35.cloned.1.call-done = bf16[64,2048]{1,0:T(8,128)(2,1)} async-done(((bf16[1024,2048]{1,0:T(8,128)(2,1)}), bf16[64,2048]{1,0:T(8,128)(2,1)}) %reduce-scatter.35.cloned.1.call-update) | async-done | bytes 262160 | tf_op jit(solution)/shard_map/while/body/eval_jaxpr/reduce_scatter | solution.py:212
  2021.8 47.5 %all-gather.15.cloned.1.call-done = bf16[2048,352]{0,1:T(8,128)(2,1)} async-done(((bf16[256,352]{0,1:T(8,128)(2,1)}), bf16[2048,352]{0,1:T(8,128)(2,1)}) %all-gather.15.cloned.1.call-update) | async-done | bytes 1441808 | tf_op jit(solution)/shard_map/while/body/eval_jaxpr/all_gather | solution.py:99
  2113.0 48.5 %all-gather.17.cloned.1.call-done = bf16[2048,352]{0,1:T(8,128)(2,1)} async-done(((bf16[256,352]{0,1:T(8,128)(2,1)}), bf16[2048,352]{0,1:T(8,128)(2,1)}) %all-gather.17.cloned.1.call-update) | async-done | bytes 1441808 | tf_op jit(solution)/shard_map/while/body/eval_jaxpr/all_gather | solution.py:100
  2220.9 65.7 %reduce-scatter.37.cloned.1.call-done = bf16[64,2048]{1,0:T(8,128)(2,1)} async-done(((bf16[1024,2048]{1,0:T(8,128)(2,1)}), bf16[64,2048]{1,0:T(8,128)(2,1)}) %reduce-scatter.37.cloned.1.call-update) | async-done | bytes 262160 | tf_op jit(solution)/shard_map/while/body/eval_jaxpr/reduce_scatter | solution.py:227
  2337.9 67.5 %reduce-scatter.39.cloned.1.call-done = bf16[64,2048]{1,0:T(8,128)(2,1)} async-done(((bf16[1024,2048]{1,0:T(8,128)(2,1)}), bf16[64,2048]{1,0:T(8,128)(2,1)}) %reduce-scatter.39.cloned.1.call-update) | async-done | bytes 262160 | tf_op jit(solution)/shard_map/while/body/eval_jaxpr/reduce_scatter | solution.py:260
  2455.1 429.0 %while.137 = (s32[]{:T(128)}, f32[1,128,128]{2,1,0:T(8,128)S(1)}, f32[16,1,64,128]{3,2,1,0:T(8,128)}, f32[16,1,64,128]{3,2,1,0:T(8,128)}, f32[16,1,64,128]{3,2,1...) while((s32[]{:T(128)}, f32[1,128,128]{2,1,0:T(8,128)S(1)}, ...), condition=%wide.region_18.19_spmd.clone, body=%wide.region_15.18_spmd.clone.sunk | while | flops 160874752 | bytes 2876935 | solution.py:80
  2997.1 66.0 %all-reduce.17 = (f32[]{:T(128)}, f32[2048]{0:T(1024)}, f32[2048]{0:T(1024)}) all-reduce(f32[]{:T(128)} %get-tuple-element.997, f32[2048]{0:T(1024)S(1)} %copy-done.68, f32[2048]{0:T(1024)S(1)} %copy-done.65), channel_id=1, replica_groups=mesh['dp'=8,'tensor'=16] {'dp','tensor'}, use_global_device_ids=true, to_apply=%region_33.35 | all-reduce | flops 4097 | bytes 32776 | tf_op jit(solution)/shard_map/psum | solution.py:317
  3110.2 71.8 %reduce-scatter.29.cloned.1.call-done = bf16[256,1]{1,0:T(8,128)(2,1)} async-done(((bf16[2048,1]{1,0:T(8,128)(2,1)}), bf16[256,1]{1,0:T(8,128)(2,1)}) %reduce-scatter.29.cloned.1.call-update) | async-done | bytes 528
  3183.5 72.5 %reduce-scatter.21.cloned.1.call-done = bf16[128,256]{1,0:T(8,128)(2,1)} async-done(((bf16[128,2048]{1,0:T(8,128)(2,1)}), bf16[128,256]{1,0:T(8,128)(2,1)}) %reduce-scatter.21.cloned.1.call-update) | async-done | bytes 65552 | tf_op jit(solution)/shard_map/reduce_scatter | solution.py:119
  3257.5 74.5 %reduce-scatter.23.cloned.1.call-done = bf16[256,352]{0,1:T(8,128)(2,1)} async-done(((bf16[2048,352]{0,1:T(8,128)(2,1)}), bf16[256,352]{0,1:T(8,128)(2,1)}) %reduce-scatter.23.cloned.1.call-update) | async-done | bytes 180240 | tf_op jit(solution)/shard_map/reduce_scatter | solution.py:122
  3333.7 74.7 %reduce-scatter.25.cloned.1.call-done = bf16[256,352]{0,1:T(8,128)(2,1)} async-done(((bf16[2048,352]{0,1:T(8,128)(2,1)}), bf16[256,352]{0,1:T(8,128)(2,1)}) %reduce-scatter.25.cloned.1.call-update) | async-done | bytes 180240 | tf_op jit(solution)/shard_map/reduce_scatter | solution.py:125
  3410.1 74.2 %reduce-scatter.27.cloned.1.call-done = bf16[352,256]{1,0:T(8,128)(2,1)} async-done(((bf16[352,2048]{1,0:T(8,128)(2,1)}), bf16[352,256]{1,0:T(8,128)(2,1)}) %reduce-scatter.27.cloned.1.call-update) | async-done | bytes 180240 | tf_op jit(solution)/shard_map/reduce_scatter | solution.py:128
  3486.0 75.3 %reduce-scatter.19.cloned.1.call-done = bf16[256,3,128]{2,0,1:T(8,128)(2,1)} async-done(((bf16[2048,3,128]{2,0,1:T(8,128)(2,1)}), bf16[256,3,128]{2,0,1:T(8,128)(2,1)}) %reduce-scatter.19.cloned.1.call-update) | async-done | bytes 196624 | tf_op jit(solution)/shard_map/reduce_scatter | solution.py:107
  (2304 shorter events, 2310.4 us)
Async XLA Ops:
  80.0 121.4 %all-gather.9.cloned.1.call-start = ((), (), s32[]{:S(2)}) async-start(), calls=%async_computation.20 | async-start | bytes 1769472 | tf_op jit(solution)/shard_map/while/body/eval_jaxpr/all_gather | solution.py:94
  80.7 120.7 %all-gather.11.cloned.1.call-start = ((), (), s32[]{:S(2)}) async-start(), calls=%async_computation.21 | async-start | bytes 4456448 | tf_op jit(solution)/shard_map/while/body/eval_jaxpr/all_gather | solution.py:195
  84.3 485.1 %reduce-scatter.35.cloned.1.call-start = ((), (), s32[]{:S(2)}) async-start(), calls=%async_computation.22 | async-start | bytes 4456448 | tf_op jit(solution)/shard_map/while/body/eval_jaxpr/reduce_scatter | solution.py:212
  504.9 116.9 %all-gather.15.cloned.1.call-start = ((), (), s32[]{:S(2)}) async-start(), calls=%async_computation.24 | async-start | bytes 1622016 | tf_op jit(solution)/shard_map/while/body/eval_jaxpr/all_gather | solution.py:99
  505.4 154.6 %all-gather.13.cloned.1.call-start = ((), (), s32[]{:S(2)}) async-start(), calls=%async_computation.23 | async-start | bytes 4456448 | tf_op jit(solution)/shard_map/while/body/eval_jaxpr/all_gather | solution.py:222
  572.5 141.5 %all-gather.17.cloned.1.call-start = ((), (), s32[]{:S(2)}) async-start(), calls=%async_computation.25 | async-start | bytes 1622016 | tf_op jit(solution)/shard_map/while/body/eval_jaxpr/all_gather | solution.py:100
  573.1 193.6 %all-gather.19.cloned.1.call-start = ((), (), s32[]{:S(2)}) async-start(), calls=%async_computation.26 | async-start | bytes 1622016 | tf_op jit(solution)/shard_map/while/body/eval_jaxpr/all_gather | solution.py:101
  573.8 265.3 %reduce-scatter.37.cloned.1.call-start = ((), (), s32[]{:S(2)}) async-start(), calls=%async_computation.27 | async-start | bytes 4456448 | tf_op jit(solution)/shard_map/while/body/eval_jaxpr/reduce_scatter | solution.py:227
  962.5 560.4 %reduce-scatter.41.cloned.1.call-start = ((), (), s32[]{:S(2)}) async-start(), calls=%async_computation.31 | async-start | bytes 4456448 | tf_op jit(solution)/shard_map/while/body/eval_jaxpr/reduce_scatter | solution.py:292
  1526.3 124.0 %all-gather.9.cloned.1.call-start = ((), (), s32[]{:S(2)}) async-start(), calls=%async_computation.20 | async-start | bytes 1769472 | tf_op jit(solution)/shard_map/while/body/eval_jaxpr/all_gather | solution.py:94
  1527.1 123.3 %all-gather.11.cloned.1.call-start = ((), (), s32[]{:S(2)}) async-start(), calls=%async_computation.21 | async-start | bytes 4456448 | tf_op jit(solution)/shard_map/while/body/eval_jaxpr/all_gather | solution.py:195
  1530.7 486.2 %reduce-scatter.35.cloned.1.call-start = ((), (), s32[]{:S(2)}) async-start(), calls=%async_computation.22 | async-start | bytes 4456448 | tf_op jit(solution)/shard_map/while/body/eval_jaxpr/reduce_scatter | solution.py:212
  1954.4 153.2 %all-gather.13.cloned.1.call-start = ((), (), s32[]{:S(2)}) async-start(), calls=%async_computation.23 | async-start | bytes 4456448 | tf_op jit(solution)/shard_map/while/body/eval_jaxpr/all_gather | solution.py:222
  2020.0 141.5 %all-gather.17.cloned.1.call-start = ((), (), s32[]{:S(2)}) async-start(), calls=%async_computation.25 | async-start | bytes 1622016 | tf_op jit(solution)/shard_map/while/body/eval_jaxpr/all_gather | solution.py:100
  2020.6 193.6 %all-gather.19.cloned.1.call-start = ((), (), s32[]{:S(2)}) async-start(), calls=%async_computation.26 | async-start | bytes 1622016 | tf_op jit(solution)/shard_map/while/body/eval_jaxpr/all_gather | solution.py:101
  2021.4 265.3 %reduce-scatter.37.cloned.1.call-start = ((), (), s32[]{:S(2)}) async-start(), calls=%async_computation.27 | async-start | bytes 4456448 | tf_op jit(solution)/shard_map/while/body/eval_jaxpr/reduce_scatter | solution.py:227
  2409.9 560.7 %reduce-scatter.41.cloned.1.call-start = ((), (), s32[]{:S(2)}) async-start(), calls=%async_computation.31 | async-start | bytes 4456448 | tf_op jit(solution)/shard_map/while/body/eval_jaxpr/reduce_scatter | solution.py:292
  2979.3 129.4 %reduce-scatter.31.cloned.1.call-start = ((), (), s32[]{:S(2)}) async-start(), calls=%async_computation.18 | async-start | bytes 36864
  2982.1 200.0 %reduce-scatter.29.cloned.1.call-start = ((), (), s32[]{:S(2)}) async-start(), calls=%async_computation.17 | async-start | bytes 589824
  2983.9 272.1 %reduce-scatter.21.cloned.1.call-start = ((), (), s32[]{:S(2)}) async-start(), calls=%async_computation.13 | async-start | bytes 589824 | tf_op jit(solution)/shard_map/reduce_scatter | solution.py:119
  2984.9 347.2 %reduce-scatter.23.cloned.1.call-start = ((), (), s32[]{:S(2)}) async-start(), calls=%async_computation.14 | async-start | bytes 1622016 | tf_op jit(solution)/shard_map/reduce_scatter | solution.py:122
  2988.1 420.3 %reduce-scatter.25.cloned.1.call-start = ((), (), s32[]{:S(2)}) async-start(), calls=%async_computation.15 | async-start | bytes 1622016 | tf_op jit(solution)/shard_map/reduce_scatter | solution.py:125
  2991.6 492.7 %reduce-scatter.27.cloned.1.call-start = ((), (), s32[]{:S(2)}) async-start(), calls=%async_computation.16 | async-start | bytes 1622016 | tf_op jit(solution)/shard_map/reduce_scatter | solution.py:128
  2993.0 568.2 %reduce-scatter.19.cloned.1.call-start = ((), (), s32[]{:S(2)}) async-start(), calls=%async_computation.12 | async-start | bytes 1769472 | tf_op jit(solution)/shard_map/reduce_scatter | solution.py:107
  (174 other events, 7654.0 us)
Sparse Core Ops, SparseCore 0:
  83.4 47.3 all-gather.8
  133.3 36.9 all-gather.10
  505.0 64.3 reduce-scatter.34
  571.6 50.0 all-gather.14
  624.0 36.0 all-gather.12
  662.4 51.6 all-gather.16
  716.4 50.2 all-gather.18
  772.9 66.1 reduce-scatter.36
  841.5 35.9 all-gather.20
  890.2 67.6 reduce-scatter.38
  962.6 35.8 all-gather.22
  1455.1 67.7 reduce-scatter.40
  1529.8 49.6 all-gather.8
  1581.8 36.8 all-gather.10
  1953.9 62.9 reduce-scatter.34
  2019.2 50.0 all-gather.14
  2071.5 36.0 all-gather.12
  2109.9 51.6 all-gather.16
  2163.9 50.2 all-gather.18
  2220.4 66.1 reduce-scatter.36
  2289.0 35.9 all-gather.20
  2337.8 67.5 reduce-scatter.38
  2410.0 36.1 all-gather.22
  2902.9 67.6 reduce-scatter.40
Sparse Core Ops, SparseCore 1:
  2982.1 60.9 reduce-scatter.32
  3047.2 61.4 reduce-scatter.30
  3112.1 69.9 reduce-scatter.28
  3186.1 69.9 reduce-scatter.20
  3259.8 72.2 reduce-scatter.22
  3336.3 72.1 reduce-scatter.24
  3412.0 72.2 reduce-scatter.26
  3488.4 72.8 reduce-scatter.18
where the time goes:
time: 3600 us; the launch traced here: 3570 us
  waiting for transfers between devices  1470 us (41%)
  other arithmetic  714 us (20%)
  matrix products  617 us (17%)
  blocking collectives  359 us (10%)
  local copies, waits for them, and re-layouts  359 us (10%)
    another operation x224, other arithmetic, delta_block(): jax.scipy.linalg.solve_triangular(matrix, right, lower=True, unit_diagona...  476 us
    reduce_scatter x2, waiting for transfers between devices, micro_step(): lax.psum_scatter((total + jnp.einsum('sf,df->sd', up_low, up_back, prefer...  135 us
    reduce_scatter x2, waiting for transfers between devices, micro_step(): lax.psum_scatter(jnp.dot(act, down_full, preferred_element_type=jnp.float...  131 us
    reduce_scatter x2, waiting for transfers between devices, micro_step(): lax.psum_scatter(jnp.dot(heads_low, out_full, preferred_element_type=jnp....  126 us
    squeeze x160, local copies, waits for them, and re-layouts, mixer(): lax.scan(jax.checkpoint(delta_block), start, (arrange(query), arrange(key...  119 us
    unnamed x11, waiting for transfers between devices  116 us
    dot_general x96, matrix products, delta_block(): jnp.einsum('hsv,hsk->hvk', weighted * closing[None, :, None], keys, preci...  108 us
    all_gather x2, waiting for transfers between devices, fetch(): lax.all_gather(up_weight, 'dp', axis=0, tiled=True)  97 us
  transfers between devices with their start and end apart: 32, of which 27 were waited for; matrix products, arithmetic and copies ran while one was open for 3% of the time, Pallas kernels for 0%

commit v1 on v0

--- a/solution.py
+++ b/solution.py
@@ -219,7 +219,9 @@
         mlp_scale = lax.rsqrt(jnp.mean(hidden * hidden, -1, keepdims=True) + 1e-06)
         mlp_unit = hidden * mlp_scale
         ffn_in = (mlp_unit * mlp_gain).astype(jnp.bfloat16)
-        ffn_all = lax.all_gather(ffn_in, "tensor", axis=0, tiled=True)
+        ffn_all = jnp.concatenate(
+            lax.all_to_all(jnp.stack([ffn_in] * lax.axis_size("tensor")), "tensor", 0, 0), axis=0
+        )
         gate = jnp.dot(ffn_all, gate_full, preferred_element_type=jnp.float32)
         up = jnp.dot(ffn_all, up_full, preferred_element_type=jnp.float32)
         sigma = jax.nn.sigmoid(gate)

time: 3600 us -> 3580 us (level)
  waiting for transfers between devices: 1470 us -> 1420 us
    all_gather x2 -> x0, waiting for transfers between devices: 76.7 us -> none  [micro_step(): ffn_all = lax.all_gather(ffn_in, 'tensor', axis=0, tiled=True)]
  transfers between devices with their start and end apart: 32 -> 32, of which waited for: 27 -> 25; matrix products, arithmetic and copies ran while one was open for 3% -> 4% of each run, Pallas kernels for 0% -> 0%
where the time goes in v1:
time: 3580 us; the launch traced here: 3560 us
  waiting for transfers between devices  1420 us (40%)
  other arithmetic  716 us (20%)
  matrix products  632 us (18%)
  local copies, waits for them, and re-layouts  366 us (10%)
  blocking collectives  359 us (10%)
    another operation x224, other arithmetic, delta_block(): jax.scipy.linalg.solve_triangular(matrix, right, lower=True, unit_diagona...  476 us
    reduce_scatter x2, waiting for transfers between devices, micro_step(): lax.psum_scatter((total + jnp.einsum('sf,df->sd', up_low, up_back, prefer...  135 us
    reduce_scatter x2, waiting for transfers between devices, micro_step(): lax.psum_scatter(jnp.dot(act, down_full, preferred_element_type=jnp.float...  131 us
    reduce_scatter x2, waiting for transfers between devices, micro_step(): lax.psum_scatter(jnp.dot(heads_low, out_full, preferred_element_type=jnp....  126 us
    all_gather x2, waiting for transfers between devices, fetch(): lax.all_gather(gate_weight, 'dp', axis=0, tiled=True)  124 us
    squeeze x160, local copies, waits for them, and re-layouts, mixer(): lax.scan(jax.checkpoint(delta_block), start, (arrange(query), arrange(key...  120 us
    unnamed x11, waiting for transfers between devices  116 us
    dot_general x96, matrix products, delta_block(): jnp.einsum('hsv,hsk->hvk', weighted * closing[None, :, None], keys, preci...  111 us
  transfers between devices with their start and end apart: 32, of which 25 were waited for; matrix products, arithmetic and copies ran while one was open for 4% of the time, Pallas kernels for 0%

profile of v1, /device:TPU:0, one launch (start us, length us, event | category | flops | bytes accessed | tf_op | source)
XLA Modules:
  0.0 3557.5 jit_solution(8500744530600312004)
XLA Ops:
  9.4 68.2 %psum.28 = s32[]{:T(128)} all-reduce(s32[]{:T(128)} %reduce_sum.286), channel_id=1, replica_groups=mesh['dp'=8,'tensor'=16] {'dp','tensor'}, use_global_device_ids=true, to_apply=%region_1.0 | all-reduce | flops 1 | bytes 8 | tf_op jit(solution)/shard_map/psum | solution.py:159
  79.7 2883.3 %while.135 = (s32[]{:T(128)}, f32[2048,3,128]{2,0,1:T(8,128)}, f32[2048,1]{0,1:T(1,128)}, f32[4,3,1,128]{3,2,1,0:T(1,128)}, f32[1,128]{1,0:T(1,128)}, /*index=5*...) while((s32[]{:T(128)}, f32[2048,3,128]{2,0,1:T(8,128)}, ...), condition=%wide.region_32.34_spmd.clone, body=%wide.region_2.33_spmd.clone.sunk | while | flops 20024219648 | bytes 537590272 | solution.py:313
  220.6 277.8 %while.136 = (s32[]{:T(128)}, f32[1,128,128]{2,1,0:T(8,128)S(1)}, s32[]{:T(128)}, f32[16,1,64,128]{3,2,1,0:T(8,128)}, f32[16,1,128,128]{3,2,1,0:T(8,128)}, /*ind...) while((s32[]{:T(128)}, f32[1,128,128]{2,1,0:T(8,128)S(1)}, ...), condition=%wide.region_7.8_spmd.clone, body=%wide.region_6.7_spmd.clone.sunk | while | flops 63140160 | bytes 960217 | solution.py:80
  506.5 63.7 %reduce-scatter.35.cloned.1.call-done = bf16[64,2048]{1,0:T(8,128)(2,1)} async-done(((bf16[1024,2048]{1,0:T(8,128)(2,1)}), bf16[64,2048]{1,0:T(8,128)(2,1)}) %reduce-scatter.35.cloned.1.call-update) | async-done | bytes 262160 | tf_op jit(solution)/shard_map/while/body/eval_jaxpr/reduce_scatter | solution.py:212
  581.3 62.0 %all-gather.12.cloned.1.call-done = bf16[2048,352]{0,1:T(8,128)(2,1)} async-done(((bf16[256,352]{0,1:T(8,128)(2,1)}), bf16[2048,352]{0,1:T(8,128)(2,1)}) %all-gather.12.cloned.1.call-update) | async-done | bytes 1441808 | tf_op jit(solution)/shard_map/while/body/eval_jaxpr/all_gather | solution.py:99
  648.8 52.7 %all-gather.14.cloned.1.call-done = bf16[2048,352]{0,1:T(8,128)(2,1)} async-done(((bf16[256,352]{0,1:T(8,128)(2,1)}), bf16[2048,352]{0,1:T(8,128)(2,1)}) %all-gather.14.cloned.1.call-update) | async-done | bytes 1441808 | tf_op jit(solution)/shard_map/while/body/eval_jaxpr/all_gather | solution.py:100
  707.7 46.4 %all-gather.16.cloned.1.call-done = bf16[352,2048]{1,0:T(8,128)(2,1)} async-done(((bf16[352,256]{1,0:T(8,128)(2,1)}), bf16[352,2048]{1,0:T(8,128)(2,1)}) %all-gather.16.cloned.1.call-update) | async-done | bytes 1441808 | tf_op jit(solution)/shard_map/while/body/eval_jaxpr/all_gather | solution.py:101
  760.8 65.7 %reduce-scatter.37.cloned.1.call-done = bf16[64,2048]{1,0:T(8,128)(2,1)} async-done(((bf16[1024,2048]{1,0:T(8,128)(2,1)}), bf16[64,2048]{1,0:T(8,128)(2,1)}) %reduce-scatter.37.cloned.1.call-update) | async-done | bytes 262160 | tf_op jit(solution)/shard_map/while/body/eval_jaxpr/reduce_scatter | solution.py:229
  878.0 67.2 %reduce-scatter.39.cloned.1.call-done = bf16[64,2048]{1,0:T(8,128)(2,1)} async-done(((bf16[1024,2048]{1,0:T(8,128)(2,1)}), bf16[64,2048]{1,0:T(8,128)(2,1)}) %reduce-scatter.39.cloned.1.call-update) | async-done | bytes 262160 | tf_op jit(solution)/shard_map/while/body/eval_jaxpr/reduce_scatter | solution.py:262
  994.8 434.5 %while.137 = (s32[]{:T(128)}, f32[1,128,128]{2,1,0:T(8,128)S(1)}, f32[16,1,64,128]{3,2,1,0:T(8,128)}, f32[16,1,64,128]{3,2,1,0:T(8,128)}, f32[16,1,64,128]{3,2,1...) while((s32[]{:T(128)}, f32[1,128,128]{2,1,0:T(8,128)S(1)}, ...), condition=%wide.region_18.19_spmd.clone, body=%wide.region_15.18_spmd.clone.sunk | while | flops 160874752 | bytes 2876935 | solution.py:80
  1662.2 277.7 %while.136 = (s32[]{:T(128)}, f32[1,128,128]{2,1,0:T(8,128)S(1)}, s32[]{:T(128)}, f32[16,1,64,128]{3,2,1,0:T(8,128)}, f32[16,1,128,128]{3,2,1,0:T(8,128)}, /*ind...) while((s32[]{:T(128)}, f32[1,128,128]{2,1,0:T(8,128)S(1)}, ...), condition=%wide.region_7.8_spmd.clone, body=%wide.region_6.7_spmd.clone.sunk | while | flops 63140160 | bytes 960217 | solution.py:80
  1948.2 62.5 %reduce-scatter.35.cloned.1.call-done = bf16[64,2048]{1,0:T(8,128)(2,1)} async-done(((bf16[1024,2048]{1,0:T(8,128)(2,1)}), bf16[64,2048]{1,0:T(8,128)(2,1)}) %reduce-scatter.35.cloned.1.call-update) | async-done | bytes 262160 | tf_op jit(solution)/shard_map/while/body/eval_jaxpr/reduce_scatter | solution.py:212
  2021.9 61.7 %all-gather.12.cloned.1.call-done = bf16[2048,352]{0,1:T(8,128)(2,1)} async-done(((bf16[256,352]{0,1:T(8,128)(2,1)}), bf16[2048,352]{0,1:T(8,128)(2,1)}) %all-gather.12.cloned.1.call-update) | async-done | bytes 1441808 | tf_op jit(solution)/shard_map/while/body/eval_jaxpr/all_gather | solution.py:99
  2089.0 52.8 %all-gather.14.cloned.1.call-done = bf16[2048,352]{0,1:T(8,128)(2,1)} async-done(((bf16[256,352]{0,1:T(8,128)(2,1)}), bf16[2048,352]{0,1:T(8,128)(2,1)}) %all-gather.14.cloned.1.call-update) | async-done | bytes 1441808 | tf_op jit(solution)/shard_map/while/body/eval_jaxpr/all_gather | solution.py:100
  2201.1 65.7 %reduce-scatter.37.cloned.1.call-done = bf16[64,2048]{1,0:T(8,128)(2,1)} async-done(((bf16[1024,2048]{1,0:T(8,128)(2,1)}), bf16[64,2048]{1,0:T(8,128)(2,1)}) %reduce-scatter.37.cloned.1.call-update) | async-done | bytes 262160 | tf_op jit(solution)/shard_map/while/body/eval_jaxpr/reduce_scatter | solution.py:229
  2317.9 67.5 %reduce-scatter.39.cloned.1.call-done = bf16[64,2048]{1,0:T(8,128)(2,1)} async-done(((bf16[1024,2048]{1,0:T(8,128)(2,1)}), bf16[64,2048]{1,0:T(8,128)(2,1)}) %reduce-scatter.39.cloned.1.call-update) | async-done | bytes 262160 | tf_op jit(solution)/shard_map/while/body/eval_jaxpr/reduce_scatter | solution.py:262
  2434.9 434.5 %while.137 = (s32[]{:T(128)}, f32[1,128,128]{2,1,0:T(8,128)S(1)}, f32[16,1,64,128]{3,2,1,0:T(8,128)}, f32[16,1,64,128]{3,2,1,0:T(8,128)}, f32[16,1,64,128]{3,2,1...) while((s32[]{:T(128)}, f32[1,128,128]{2,1,0:T(8,128)S(1)}, ...), condition=%wide.region_18.19_spmd.clone, body=%wide.region_15.18_spmd.clone.sunk | while | flops 160874752 | bytes 2876935 | solution.py:80
  2982.4 66.1 %all-reduce.17 = (f32[]{:T(128)}, f32[2048]{0:T(1024)}, f32[2048]{0:T(1024)}) all-reduce(f32[]{:T(128)} %get-tuple-element.997, f32[2048]{0:T(1024)S(1)} %copy-done.66, f32[2048]{0:T(1024)S(1)} %copy-done.63), channel_id=1, replica_groups=mesh['dp'=8,'tensor'=16] {'dp','tensor'}, use_global_device_ids=true, to_apply=%region_33.35 | all-reduce | flops 4097 | bytes 32776 | tf_op jit(solution)/shard_map/psum | solution.py:319
  3095.6 71.8 %reduce-scatter.29.cloned.1.call-done = bf16[256,1]{1,0:T(8,128)(2,1)} async-done(((bf16[2048,1]{1,0:T(8,128)(2,1)}), bf16[256,1]{1,0:T(8,128)(2,1)}) %reduce-scatter.29.cloned.1.call-update) | async-done | bytes 528
  3168.9 72.5 %reduce-scatter.21.cloned.1.call-done = bf16[128,256]{1,0:T(8,128)(2,1)} async-done(((bf16[128,2048]{1,0:T(8,128)(2,1)}), bf16[128,256]{1,0:T(8,128)(2,1)}) %reduce-scatter.21.cloned.1.call-update) | async-done | bytes 65552 | tf_op jit(solution)/shard_map/reduce_scatter | solution.py:119
  3242.9 74.6 %reduce-scatter.23.cloned.1.call-done = bf16[256,352]{0,1:T(8,128)(2,1)} async-done(((bf16[2048,352]{0,1:T(8,128)(2,1)}), bf16[256,352]{0,1:T(8,128)(2,1)}) %reduce-scatter.23.cloned.1.call-update) | async-done | bytes 180240 | tf_op jit(solution)/shard_map/reduce_scatter | solution.py:122
  3319.2 74.7 %reduce-scatter.25.cloned.1.call-done = bf16[256,352]{0,1:T(8,128)(2,1)} async-done(((bf16[2048,352]{0,1:T(8,128)(2,1)}), bf16[256,352]{0,1:T(8,128)(2,1)}) %reduce-scatter.25.cloned.1.call-update) | async-done | bytes 180240 | tf_op jit(solution)/shard_map/reduce_scatter | solution.py:125
  3395.6 74.1 %reduce-scatter.27.cloned.1.call-done = bf16[352,256]{1,0:T(8,128)(2,1)} async-done(((bf16[352,2048]{1,0:T(8,128)(2,1)}), bf16[352,256]{1,0:T(8,128)(2,1)}) %reduce-scatter.27.cloned.1.call-update) | async-done | bytes 180240 | tf_op jit(solution)/shard_map/reduce_scatter | solution.py:128
  3471.4 75.4 %reduce-scatter.19.cloned.1.call-done = bf16[256,3,128]{2,0,1:T(8,128)(2,1)} async-done(((bf16[2048,3,128]{2,0,1:T(8,128)(2,1)}), bf16[256,3,128]{2,0,1:T(8,128)(2,1)}) %reduce-scatter.19.cloned.1.call-update) | async-done | bytes 196624 | tf_op jit(solution)/shard_map/reduce_scatter | solution.py:107
  (2292 shorter events, 2259.2 us)
Async XLA Ops:
  80.0 121.5 %all-gather.8.cloned.1.call-start = ((), (), s32[]{:S(2)}) async-start(), calls=%async_computation.21 | async-start | bytes 1769472 | tf_op jit(solution)/shard_map/while/body/eval_jaxpr/all_gather | solution.py:94
  80.7 120.7 %all-gather.10.cloned.1.call-start = ((), (), s32[]{:S(2)}) async-start(), calls=%async_computation.22 | async-start | bytes 4456448 | tf_op jit(solution)/shard_map/while/body/eval_jaxpr/all_gather | solution.py:195
  84.3 486.0 %reduce-scatter.35.cloned.1.call-start = ((), (), s32[]{:S(2)}) async-start(), calls=%async_computation.23 | async-start | bytes 4456448 | tf_op jit(solution)/shard_map/while/body/eval_jaxpr/reduce_scatter | solution.py:212
  506.0 137.4 %all-gather.12.cloned.1.call-start = ((), (), s32[]{:S(2)}) async-start(), calls=%async_computation.24 | async-start | bytes 1622016 | tf_op jit(solution)/shard_map/while/body/eval_jaxpr/all_gather | solution.py:99
  579.8 121.7 %all-gather.14.cloned.1.call-start = ((), (), s32[]{:S(2)}) async-start(), calls=%async_computation.25 | async-start | bytes 1622016 | tf_op jit(solution)/shard_map/while/body/eval_jaxpr/all_gather | solution.py:100
  580.4 173.6 %all-gather.16.cloned.1.call-start = ((), (), s32[]{:S(2)}) async-start(), calls=%async_computation.26 | async-start | bytes 1622016 | tf_op jit(solution)/shard_map/while/body/eval_jaxpr/all_gather | solution.py:101
  581.0 245.5 %reduce-scatter.37.cloned.1.call-start = ((), (), s32[]{:S(2)}) async-start(), calls=%async_computation.27 | async-start | bytes 4456448 | tf_op jit(solution)/shard_map/while/body/eval_jaxpr/reduce_scatter | solution.py:229
  828.5 116.7 %reduce-scatter.39.cloned.1.call-start = ((), (), s32[]{:S(2)}) async-start(), calls=%async_computation.29 | async-start | bytes 4456448 | tf_op jit(solution)/shard_map/while/body/eval_jaxpr/reduce_scatter | solution.py:262
  949.7 566.1 %reduce-scatter.41.cloned.1.call-start = ((), (), s32[]{:S(2)}) async-start(), calls=%async_computation.31 | async-start | bytes 4456448 | tf_op jit(solution)/shard_map/while/body/eval_jaxpr/reduce_scatter | solution.py:294
  1519.3 123.8 %all-gather.8.cloned.1.call-start = ((), (), s32[]{:S(2)}) async-start(), calls=%async_computation.21 | async-start | bytes 1769472 | tf_op jit(solution)/shard_map/while/body/eval_jaxpr/all_gather | solution.py:94
  1519.9 123.2 %all-gather.10.cloned.1.call-start = ((), (), s32[]{:S(2)}) async-start(), calls=%async_computation.22 | async-start | bytes 4456448 | tf_op jit(solution)/shard_map/while/body/eval_jaxpr/all_gather | solution.py:195
  1523.5 487.2 %reduce-scatter.35.cloned.1.call-start = ((), (), s32[]{:S(2)}) async-start(), calls=%async_computation.23 | async-start | bytes 4456448 | tf_op jit(solution)/shard_map/while/body/eval_jaxpr/reduce_scatter | solution.py:212
  1947.6 135.9 %all-gather.12.cloned.1.call-start = ((), (), s32[]{:S(2)}) async-start(), calls=%async_computation.24 | async-start | bytes 1622016 | tf_op jit(solution)/shard_map/while/body/eval_jaxpr/all_gather | solution.py:99
  2020.3 121.6 %all-gather.14.cloned.1.call-start = ((), (), s32[]{:S(2)}) async-start(), calls=%async_computation.25 | async-start | bytes 1622016 | tf_op jit(solution)/shard_map/while/body/eval_jaxpr/all_gather | solution.py:100
  2020.8 173.5 %all-gather.16.cloned.1.call-start = ((), (), s32[]{:S(2)}) async-start(), calls=%async_computation.26 | async-start | bytes 1622016 | tf_op jit(solution)/shard_map/while/body/eval_jaxpr/all_gather | solution.py:101
  2021.4 245.4 %reduce-scatter.37.cloned.1.call-start = ((), (), s32[]{:S(2)}) async-start(), calls=%async_computation.27 | async-start | bytes 4456448 | tf_op jit(solution)/shard_map/while/body/eval_jaxpr/reduce_scatter | solution.py:229
  2390.0 565.9 %reduce-scatter.41.cloned.1.call-start = ((), (), s32[]{:S(2)}) async-start(), calls=%async_computation.31 | async-start | bytes 4456448 | tf_op jit(solution)/shard_map/while/body/eval_jaxpr/reduce_scatter | solution.py:294
  2964.6 129.5 %reduce-scatter.31.cloned.1.call-start = ((), (), s32[]{:S(2)}) async-start(), calls=%async_computation.19 | async-start | bytes 36864
  2967.4 200.0 %reduce-scatter.29.cloned.1.call-start = ((), (), s32[]{:S(2)}) async-start(), calls=%async_computation.18 | async-start | bytes 589824
  2969.2 272.2 %reduce-scatter.21.cloned.1.call-start = ((), (), s32[]{:S(2)}) async-start(), calls=%async_computation.14 | async-start | bytes 589824 | tf_op jit(solution)/shard_map/reduce_scatter | solution.py:119
  2970.2 347.3 %reduce-scatter.23.cloned.1.call-start = ((), (), s32[]{:S(2)}) async-start(), calls=%async_computation.15 | async-start | bytes 1622016 | tf_op jit(solution)/shard_map/reduce_scatter | solution.py:122
  2973.6 420.3 %reduce-scatter.25.cloned.1.call-start = ((), (), s32[]{:S(2)}) async-start(), calls=%async_computation.16 | async-start | bytes 1622016 | tf_op jit(solution)/shard_map/reduce_scatter | solution.py:125
  2975.1 494.6 %reduce-scatter.27.cloned.1.call-start = ((), (), s32[]{:S(2)}) async-start(), calls=%async_computation.17 | async-start | bytes 1622016 | tf_op jit(solution)/shard_map/reduce_scatter | solution.py:128
  2978.3 568.4 %reduce-scatter.19.cloned.1.call-start = ((), (), s32[]{:S(2)}) async-start(), calls=%async_computation.13 | async-start | bytes 1769472 | tf_op jit(solution)/shard_map/reduce_scatter | solution.py:107
  (168 other events, 7469.2 us)
Sparse Core Ops, SparseCore 0:
  83.4 47.3 all-gather.7
  133.2 36.7 all-gather.9
  506.1 64.1 reduce-scatter.34
  572.6 70.7 all-gather.11
  645.6 55.8 all-gather.13
  703.8 50.2 all-gather.15
  760.2 66.1 reduce-scatter.36
  828.9 35.9 all-gather.17
  877.6 67.5 reduce-scatter.38
  949.8 36.1 all-gather.19
  1448.2 67.6 reduce-scatter.40
  1522.5 49.8 all-gather.7
  1574.8 36.7 all-gather.9
  1947.8 62.9 reduce-scatter.34
  2013.0 70.5 all-gather.11
  2085.9 55.9 all-gather.13
  2144.1 50.2 all-gather.15
  2200.6 66.2 reduce-scatter.36
  2269.2 35.8 all-gather.17
  2317.8 67.5 reduce-scatter.38
  2390.1 36.0 all-gather.19
  2888.3 67.5 reduce-scatter.40
Sparse Core Ops, SparseCore 1:
  2967.4 60.9 reduce-scatter.32
  3032.6 61.4 reduce-scatter.30
  3097.5 69.9 reduce-scatter.28
  3171.4 69.9 reduce-scatter.20
  3245.2 72.3 reduce-scatter.22
  3321.7 72.1 reduce-scatter.24
  3397.5 72.1 reduce-scatter.26
  3473.8 72.9 reduce-scatter.18
